TPU v7x, 32 devices: a whole 2x2x4 slice. The times are simulated.
32 devices in a mesh: section: 2 (over x), tensor: 16 (over z, y, core).
Axes of the slice: x: 2, y: 2, z: 4, core: 2. Of those that a mesh axis runs over, the one named last changes fastest.
Arguments:
- patches: bfloat16 [128, 1280], P(('section', 'tensor')), may hold values from -6 to 6
- intermediate: bfloat16 [128, 6400], P(('section', 'tensor')), may hold values from -6 to 6
- fc1_weight: bfloat16 [1280, 5120], P(None, 'tensor'), may hold values from -0.15625 to 0.15625
- fc2_weight: bfloat16 [5120, 1280], P('tensor'), may hold values from -0.078125 to 0.078125
- projector: bfloat16 [7680, 8192], P(None, 'tensor'), may hold values from -0.0625 to 0.0625
- text: bfloat16 [2, 256, 8192], P('section', None, 'tensor'), may hold values from -6 to 6
- query_weight: bfloat16 [2, 8192, 8192], P('section', None, 'tensor'), may hold values from -0.0625 to 0.0625
- kv_weight: bfloat16 [2, 8192, 2048], P('section', 'tensor'), may hold values from -0.0625 to 0.0625
- query_gain: float32 [2, 128], P('section')
- key_gain: float32 [2, 128], P('section')
- out_weight: bfloat16 [2, 8192, 8192], P('section', 'tensor'), may hold values from -0.09375 to 0.09375
- attn_gate: float32 [2], P('section'), may hold values from 0.4 to 1.4
- tile_list: int32 [2, 4, 4], P('section'), may hold values from 0 to 1
- list_count: int32 [2, 4], P('section'), may hold values from 1 to 4, as said below
Outputs:
- mixed: bfloat16 [2, 256, 8192], P('section', None, 'tensor')
Inputs may be any that keep to these rules, and one draw needn't show every extreme that they name: `list_count`: some block has 4 used slots and some has one; tiles may repeat within a list.
All inputs are finite; a program needn't handle non-finite values.
Results may differ from a plain program's by a relative error of at most 0.017.
The roundings to bfloat16 on the way count: a program that leaves them out, or rounds other values in their place, can miss the bound.
Values may be sent and summed in bfloat16 or wider, within the bound.
A program may use at most 128 MiB of HBM per device.

v0:
```python
import jax
import jax.numpy as jnp
from jax import lax
from jax.sharding import PartitionSpec as P

HEADS = 64
KV_HEADS = 8
HD = 128
TILE_ROWS = 64
TBLOCK = 64


def layer_norm(values):
    center = values - jnp.mean(values, axis=-1, keepdims=True)
    spread = jnp.mean(center * center, axis=-1, keepdims=True)
    return center * lax.rsqrt(spread + 1e-06)


def rms_scale(values, gain):
    return values * lax.rsqrt(jnp.mean(values * values, axis=-1, keepdims=True) + 1e-05) * gain


def visible_rows(tiles, counts, tile_total):
    slots = jnp.arange(tiles.shape[1], dtype=jnp.int32)
    used = slots[None, :] < counts[:, None]
    targets = jnp.arange(tile_total, dtype=jnp.int32)
    hits = (tiles[:, :, None] == targets[None, None, :]) & used[:, :, None]
    allowed = jnp.any(hits, axis=1)
    key_ok = jnp.repeat(allowed, TILE_ROWS, axis=1)
    return jnp.repeat(key_ok, TBLOCK, axis=0)


def shards(
    patches,
    intermediate,
    fc1_weight,
    fc2_weight,
    projector,
    text,
    query_weight,
    kv_weight,
    query_gain,
    key_gain,
    out_weight,
    attn_gate,
    tile_list,
    list_count,
):
    group_rows, group_inter = (
        lax.all_gather(patches, "tensor", axis=0, tiled=True),
        lax.all_gather(intermediate, "tensor", axis=0, tiled=True),
    )
    states = group_rows.astype(jnp.float32)
    normed = layer_norm(states).astype(jnp.bfloat16)
    hidden = jax.nn.gelu(
        jnp.dot(normed, fc1_weight, preferred_element_type=jnp.float32), approximate=False
    ).astype(jnp.bfloat16)
    partial_value = jnp.dot(hidden, fc2_weight, preferred_element_type=jnp.float32)
    encoded = (states + lax.psum(partial_value, "tensor")).astype(jnp.bfloat16)
    enc_width = encoded.shape[1]
    image_sum = jnp.dot(encoded, projector[:enc_width], preferred_element_type=jnp.float32)
    image_sum = image_sum + jnp.dot(
        group_inter, projector[enc_width:], preferred_element_type=jnp.float32
    )
    image_cols = image_sum.astype(jnp.bfloat16)
    image_all = lax.all_gather(image_cols, "section", axis=0, tiled=True)
    kv_local = kv_weight[0]
    image_total = image_all.shape[0]
    key_width = KV_HEADS * HD
    heads_local = query_weight.shape[2] // HD
    head_first = lax.axis_index("tensor") * heads_local
    key_head = head_first // (HEADS // KV_HEADS)
    own_kv = lax.psum_scatter(
        jnp.dot(image_all, kv_local, preferred_element_type=jnp.float32),
        "tensor",
        scatter_dimension=0,
        tiled=True,
    ).astype(jnp.bfloat16)
    kv_all = lax.all_gather(own_kv, "tensor", axis=0, tiled=True)
    keys = lax.dynamic_slice_in_dim(kv_all, key_head * HD, HD, 1).astype(jnp.float32)
    values = lax.dynamic_slice_in_dim(kv_all, key_width + key_head * HD, HD, 1)
    key_normed = rms_scale(keys, key_gain[0]).astype(jnp.bfloat16)
    full_text = lax.all_gather(text[0], "tensor", axis=1, tiled=True)
    rows_text = full_text.shape[0]
    query = jnp.dot(full_text, query_weight[0], preferred_element_type=jnp.float32).reshape(
        rows_text, heads_local, HD
    )
    query_normed = rms_scale(query, query_gain[0]).astype(jnp.bfloat16)
    scores = jnp.einsum(
        "thd,kd->htk", query_normed, key_normed, preferred_element_type=jnp.float32
    ) * (1.0 / HD**0.5)
    row_ok = visible_rows(tile_list[0], list_count[0], image_total // TILE_ROWS)
    scores = jnp.where(row_ok[None], scores, -1e30)
    top = jnp.max(scores, axis=-1, keepdims=True)
    weights = jnp.exp(scores - top)
    probs = (weights / jnp.sum(weights, axis=-1, keepdims=True)).astype(jnp.bfloat16)
    attended = jnp.einsum("htk,kd->thd", probs, values, preferred_element_type=jnp.float32).astype(
        jnp.bfloat16
    )
    attended = attended.reshape(rows_text, heads_local * HD)
    terms = jnp.dot(attended, out_weight[0], preferred_element_type=jnp.float32)
    branch = lax.psum_scatter(terms, "tensor", scatter_dimension=1, tiled=True)
    mixed = text[0].astype(jnp.float32) + jnp.tanh(attn_gate[0]) * branch
    return mixed.astype(jnp.bfloat16)[None]


def solution(mesh):
    placed = (
        P(("section", "tensor"), None),
        P(("section", "tensor"), None),
        P(None, "tensor"),
        P("tensor", None),
        P(None, "tensor"),
        P("section", None, "tensor"),
        P("section", None, "tensor"),
        P("section", "tensor", None),
        P("section", None),
        P("section", None),
        P("section", "tensor", None),
        P("section"),
        P("section", None, None),
        P("section", None),
    )
    return jax.shard_map(
        shards, mesh=mesh, in_specs=placed, out_specs=P("section", None, "tensor"), check_vma=False
    )
```

profile of v0, /device:TPU:0, one launch (start us, length us, event | category | flops | bytes accessed | tf_op | source)
XLA Modules:
  0.0 371.4 jit_solution(17204455670070767149)
XLA Ops:
  6.5 0.0 copy-start
  6.5 0.0 all-reduce.2.cloned.1.call-start
  6.5 23.9 %all-gather.1 = bf16[16,4,1280]{2,1,0:T(4,128)(2,1)S(1)} all-gather(bf16[1,4,1280]{2,1,0:T(4,128)(2,1)} %bitcast.55), channel_id=1, replica_groups=mesh['section'=2,'tensor'=16] {'tensor'}, dimensions={0}, use_global_device_ids=true | all-gather | bytes 174080 | tf_op jit(solution)/shard_map/all_gather | solution.py:50
  30.5 0.1 convert_reduce_fusion
  30.6 0.1 reshape.77
  30.7 0.2 multiply_reduce_fusion.1
  30.9 3.1 fusion.38
  34.0 0.0 all-reduce.2.cloned.1.call-update
  34.0 0.0 reduce-scatter.3.cloned.1.call-start
  34.1 20.5 %all-gather.2 = bf16[16,4,6400]{2,1,0:T(4,128)(2,1)S(1)} all-gather(bf16[1,4,6400]{2,1,0:T(4,128)(2,1)} %bitcast.54), channel_id=1, replica_groups=mesh['section'=2,'tensor'=16] {'tensor'}, dimensions={0}, use_global_device_ids=true | all-gather | bytes 870400 | tf_op jit(solution)/shard_map/all_gather | solution.py:51
  54.6 1.1 reshape.73
  55.7 4.4 %fusion.3 = f32[64,512]{1,0:T(8,128)S(1)} fusion(bf16[64,6400]{1,0:T(8,128)(2,1)} %reshape.73, bf16[7680,512]{1,0:T(8,128)(2,1)} %param.18), kind=kOutput, calls=%fused_computation.3 | convolution fusion | flops 419430400 | bytes 7503872 | tf_op jit(solution)/shard_map/dot_general | solution.py:62
  60.1 60.7 %all-reduce.2.cloned.1.call-done = f32[64,1280]{1,0:T(8,128)} async-done(((f32[64,1280]{1,0:T(8,128)}), f32[64,1280]{1,0:T(8,128)}) %all-reduce.2.cloned.1.call-update) | async-done | bytes 327696 | tf_op jit(solution)/shard_map/psum | solution.py:59
  120.8 1.8 fusion.18
  122.6 5.1 %all_gather.17 = bf16[128,512]{1,0:T(8,128)(2,1)S(1)} all-gather(bf16[64,512]{1,0:T(8,128)(2,1)S(1)} %fusion.18), channel_id=1, replica_groups=mesh['section'=2,'tensor'=16] {'section'}, dimensions={0}, use_global_device_ids=true | all-gather | bytes 196608 | tf_op jit(solution)/shard_map/all_gather | solution.py:66
  127.7 0.0 copy-done
  127.7 1.5 fusion.7
  129.2 0.0 reduce-scatter.3.cloned.1.call-update
  129.2 0.0 all-gather.5.cloned.1.call-start
  129.2 0.7 all-gather.5.cloned.1.call-update
  129.9 0.0 reduce-scatter.5.cloned.1.call-start
  130.0 0.0 copy-start.5
  130.0 0.0 copy-start.2
  130.0 11.4 %copy.44 = bf16[512,8192]{1,0:T(8,128)(2,1)} copy(bf16[512,8192]{0,1:T(8,128)(2,1)} %bitcast.50) | data formatting | bytes 16777216 | tf_op jit(solution)/shard_map/dot_general | solution.py:85
  141.4 0.0 copy-done.5
  141.4 0.1 iota_compare_fusion.1
  141.5 0.0 copy-done.2
  141.5 0.1 fusion.80
  141.7 0.1 copy.34
  141.8 0.1 broadcast_in_dim.32
  141.9 0.1 reshape.66
  142.0 0.1 copy.35
  142.1 45.5 %reduce-scatter.3.cloned.1.call-done = f32[8,2048]{1,0:T(8,128)} async-done(((f32[128,2048]{1,0:T(8,128)}), f32[8,2048]{1,0:T(8,128)}) %reduce-scatter.3.cloned.1.call-update) | async-done | bytes 65552 | tf_op jit(solution)/shard_map/reduce_scatter | solution.py:73
  187.6 0.8 convert_element_type.48
  188.5 21.5 %all_gather.18 = bf16[128,2048]{1,0:T(8,128)(2,1)S(1)} all-gather(bf16[8,2048]{1,0:T(8,128)(2,1)S(1)} %convert_element_type.48), channel_id=1, replica_groups=mesh['section'=2,'tensor'=16] {'tensor'}, dimensions={0}, use_global_device_ids=true | all-gather | bytes 557056 | tf_op jit(solution)/shard_map/all_gather | solution.py:79
  209.9 0.1 fusion.39
  210.1 33.0 %all-gather.5.cloned.1.call-done = bf16[1,256,8192]{2,1,0:T(8,128)(2,1)} async-done(((bf16[1,256,512]{2,1,0:T(8,128)(2,1)}), bf16[1,256,8192]{2,1,0:T(8,128)(2,1)}) %all-gather.5.cloned.1.call-update) | async-done | bytes 4194320 | tf_op jit(solution)/shard_map/all_gather | solution.py:83
  243.0 0.0 copy-start.3
  243.0 0.0 copy-start.4
  243.0 7.1 %multiply_reduce_fusion = (f32[256,4]{0,1:T(4,128)S(1)}, f32[256,4,128]{0,2,1:T(8,128)S(1)}) fusion(bf16[4,128,8192]{2,1,0:T(8,128)(2,1)} %bitcast.51, bf16[1,256,8192]{2,1,0:T(8,128)(2,1)} %all-gather.5.cloned.1.call-done), kind=kOutput, calls=%fused_computation.23 | convolution fusion | flops 2147744768 | bytes 13111296 | tf_op jit(solution)/shard_map/dot_general | solution.py:85
  250.1 0.0 copy-done.3
  250.1 0.0 copy-done.4
  250.1 0.3 fusion.14
  250.4 0.1 fusion.114
  250.5 0.3 convolution_convert_fusion
  250.9 9.0 %fusion.1 = f32[256,8192]{1,0:T(8,128)} fusion(bf16[256,512]{0,1:T(8,128)(2,1)S(1)} %bitcast.52, bf16[1,512,8192]{2,1,0:T(8,128)(2,1)} %param.24), kind=kOutput, calls=%fused_computation.1 | convolution fusion | flops 2147483648 | bytes 17039360 | tf_op jit(solution)/shard_map/dot_general | solution.py:101
  259.8 0.0 copy-start.1
  259.8 0.0 reduce-scatter.5.cloned.1.call-update
  260.6 102.4 %reduce-scatter.5.cloned.1.call-done = f32[256,512]{1,0:T(8,128)} async-done(((f32[256,8192]{1,0:T(8,128)}), f32[256,512]{1,0:T(8,128)}) %reduce-scatter.5.cloned.1.call-update) | async-done | bytes 524304 | tf_op jit(solution)/shard_map/reduce_scatter | solution.py:102
  363.0 0.0 copy-done.1
  363.0 1.8 fusion.22
  (6 shorter events, 0.1 us)
Async XLA Ops:
  6.5 121.1 %copy-start = (bf16[1,512,2048]{2,1,0:T(8,128)(2,1)S(1)}, bf16[1,512,2048]{2,1,0:T(8,128)(2,1)}, u32[]{:S(2)}) copy-start(bf16[1,512,2048]{2,1,0:T(8,128)(2,1)} %param.21) | copy-start | bytes 6291460
  6.5 114.3 %all-reduce.2.cloned.1.call-start = ((), (), s32[]{:S(2)}) async-start(), calls=%async_computation.2 | async-start | bytes 655360 | tf_op jit(solution)/shard_map/psum | solution.py:59
  34.0 153.6 %reduce-scatter.3.cloned.1.call-start = ((), (), s32[]{:S(2)}) async-start(), calls=%async_computation.3 | async-start | bytes 1114112 | tf_op jit(solution)/shard_map/reduce_scatter | solution.py:73
  129.2 113.8 %all-gather.5.cloned.1.call-start = ((), (), s32[]{:S(2)}) async-start(), calls=%async_computation.5 | async-start | bytes 4456448 | tf_op jit(solution)/shard_map/all_gather | solution.py:83
  129.9 233.1 %reduce-scatter.5.cloned.1.call-start = ((), (), s32[]{:S(2)}) async-start(), calls=%async_computation.4 | async-start | bytes 8912896 | tf_op jit(solution)/shard_map/reduce_scatter | solution.py:102
  130.0 11.5 %copy-start.5 = (s32[1,4]{1,0:T(1,128)S(1)}, s32[1,4]{1,0:T(1,128)}, u32[]{:S(2)}) copy-start(s32[1,4]{1,0:T(1,128)} %param.27) | copy-start | bytes 52
  130.0 11.5 %copy-start.2 = (s32[1,4,4]{2,1,0:T(4,128)S(1)}, s32[1,4,4]{2,1,0:T(4,128)}, u32[]{:S(2)}) copy-start(s32[1,4,4]{2,1,0:T(4,128)} %param.26) | copy-start | bytes 196
  243.0 7.1 %copy-start.3 = (f32[1,128]{1,0:T(1,128)S(1)}, f32[1,128]{1,0:T(1,128)}, u32[]{:S(2)}) copy-start(f32[1,128]{1,0:T(1,128)} %param.22) | copy-start | bytes 1540
  243.0 7.1 %copy-start.4 = (f32[1,128]{1,0:T(1,128)S(1)}, f32[1,128]{1,0:T(1,128)}, u32[]{:S(2)}) copy-start(f32[1,128]{1,0:T(1,128)} %param.23) | copy-start | bytes 1540
  259.8 103.2 %copy-start.1 = (bf16[1,256,512]{2,1,0:T(8,128)(2,1)S(1)}, bf16[1,256,512]{2,1,0:T(8,128)(2,1)}, u32[]{:S(2)}) copy-start(bf16[1,256,512]{2,1,0:T(8,128)(2,1)} %param.19) | copy-start | bytes 786436
Sparse Core Ops, SparseCore 0:
  34.2 86.6 all-reduce.1
  129.3 58.2 reduce-scatter.2
  189.8 53.1 all-gather.4
  260.0 103.0 reduce-scatter.4
where the time goes:
time: 372 us; the launch traced here: 371 us
  waiting for transfers between devices  242 us (65%)
  blocking collectives  71 us (19%)
  matrix products  27.4 us (7%)
  between operations  14 us (4%)
  local copies, waits for them, and re-layouts  13.1 us (4%)
    reduce_scatter x1, waiting for transfers between devices, shards(): branch = lax.psum_scatter(terms, 'tensor', scatter_dimension=1, tiled=True)  102 us
    psum x1, waiting for transfers between devices, shards(): encoded = (states + lax.psum(partial_value, 'tensor')).astype(jnp.bfloat16)  60.7 us
    reduce_scatter x1, waiting for transfers between devices, shards(): lax.psum_scatter(jnp.dot(image_all, kv_local, preferred_element_type=jnp....  45.5 us
    all_gather x1, waiting for transfers between devices, shards(): full_text = lax.all_gather(text[0], 'tensor', axis=1, tiled=True)  33 us
    all_gather x1, blocking collectives, shards(): lax.all_gather(patches, 'tensor', axis=0, tiled=True)  23.9 us
    all_gather x1, blocking collectives, shards(): kv_all = lax.all_gather(own_kv, 'tensor', axis=0, tiled=True)  21.5 us
    all_gather x1, blocking collectives, shards(): lax.all_gather(intermediate, 'tensor', axis=0, tiled=True)  20.5 us
    dot_general x1, local copies, waits for them, and re-layouts, shards(): jnp.dot(full_text, query_weight[0], preferred_element_type=jnp.float32)  11.4 us
  transfers between devices with their start and end apart: 4, of which 4 were waited for; matrix products, arithmetic and copies ran while one was open for 5% of the time, Pallas kernels for 0%

commit v1 on v0

v1 whole, which is shorter than its diff:
```python
import functools

import jax
import jax.numpy as jnp
from jax import lax
from jax.experimental import pallas as pl
from jax.experimental.pallas import tpu as pltpu
from jax.sharding import PartitionSpec as P

HEADS = 64
KV_HEADS = 8
HD = 128
TILE_ROWS = 64
TBLOCK = 64
F32 = jnp.float32
BF16 = jnp.bfloat16


def dot(a, b):
    return jnp.dot(a, b, preferred_element_type=F32)


def remote(src, dst, send, recv, **axes):
    return pltpu.make_async_remote_copy(
        src_ref=src,
        dst_ref=dst,
        send_sem=send,
        recv_sem=recv,
        device_id=axes,
        device_id_type=pl.DeviceIdType.MESH,
    )


def rms_scale(values, gain):
    return values * lax.rsqrt(jnp.mean(values * values, axis=-1, keepdims=True) + 1e-05) * gain


def each(first, last, body):
    def step(i, carry):
        body(i)
        return carry

    lax.fori_loop(first, last, step, 0)


def kernel(
    T,
    patches,
    inter,
    qgain,
    kgain,
    gate,
    tiles,
    counts,
    text,
    fc1_hbm,
    fc2_hbm,
    proj_hbm,
    qw_hbm,
    kvw_hbm,
    ow_hbm,
    out,
    fc1,
    fc2,
    proj,
    qw,
    kvw,
    ow,
    xr,
    xs,
    part,
    partr,
    er,
    ir,
    feats,
    img,
    tall,
    query,
    kvp,
    kcr,
    kzr,
    kvh,
    mask,
    att,
    ocs,
    ocr,
    own,
    oys,
    oyr,
    ozs,
    ozr,
    loc,
    xsem,
    rsem,
    esem,
    tz,
    ty,
    tc,
    iz,
    iy,
    ic,
    msem,
    kc,
    kz,
    kg,
    oc,
    oy,
    oz,
):
    A = T // 4
    J = T // 2
    G = T // KV_HEADS
    me = lax.axis_index("tensor")
    sec = lax.axis_index("section")
    z = me // 4
    y = (me // 2) % 2
    c = me % 2
    mj = me // 2
    pair = me + 1 - 2 * c
    across = me + 2 - 4 * y
    rows = patches.shape[0]
    group = T * rows
    dv = patches.shape[1]
    txt = tall.shape[1]
    width = tall.shape[2]
    hl = width // HD

    barrier = pltpu.get_barrier_semaphore()

    def greet(p):
        pl.semaphore_signal(
            barrier,
            inc=1,
            device_id={"tensor": (me + p) % T},
            device_id_type=pl.DeviceIdType.MESH,
        )

    each(1, T, greet)
    pl.semaphore_signal(
        barrier, inc=1, device_id={"section": 1 - sec}, device_id_type=pl.DeviceIdType.MESH
    )
    locals_ = [
        pltpu.make_async_copy(src, dst, loc.at[i])
        for i, (src, dst) in enumerate(
            (
                (text, tall.at[me]),
                (fc1_hbm, fc1),
                (fc2_hbm, fc2),
                (proj_hbm, proj),
                (kvw_hbm, kvw),
                (qw_hbm, qw),
                (ow_hbm, ow),
            )
        )
    ]
    for copy in locals_:
        copy.start()
    xr[me] = patches[...]
    ir[me] = inter[...]
    pl.semaphore_wait(barrier, T)

    def spread(buf, sem, p):
        return remote(
            buf.at[me], buf.at[me], sem.at[0, p], sem.at[1, me], tensor=(me + p) % T
        )

    def spread_in(buf, sem, p):
        src = (me + p) % T
        return remote(buf.at[src], buf.at[src], sem.at[0, p], sem.at[1, src], tensor=src)

    def part_out(p):
        to = (me + p) % T
        return remote(part.at[to], partr.at[me], rsem.at[0, p], rsem.at[1, me], tensor=to)

    def part_in(p):
        src = (me + p) % T
        return remote(part.at[src], partr.at[src], rsem.at[0, p], rsem.at[1, src], tensor=src)

    def line(buf, sem, p):
        to = ((z + p) % A) * 4 + y * 2 + c
        return remote(buf.at[me], buf.at[me], sem.at[0, p], sem.at[1, z], tensor=to)

    def line_in(buf, sem, p):
        zs = (z + p) % A
        src = zs * 4 + y * 2 + c
        return remote(buf.at[src], buf.at[src], sem.at[0, p], sem.at[1, zs], tensor=src)

    def cross(buf, sem, zs):
        b = zs * 4 + y * 2 + c
        return remote(buf.at[b], buf.at[b], sem.at[0, zs], sem.at[1, zs], tensor=across)

    def cross_in(buf, sem, zs):
        b = zs * 4 + (1 - y) * 2 + c
        return remote(buf.at[b], buf.at[b], sem.at[0, zs], sem.at[1, zs], tensor=across)

    def core(buf, sem, j):
        b = j * 2 + c
        return remote(buf.at[b], buf.at[b], sem.at[0, j], sem.at[1, j], tensor=pair)

    def core_in(buf, sem, j):
        b = j * 2 + 1 - c
        return remote(buf.at[b], buf.at[b], sem.at[0, j], sem.at[1, j], tensor=pair)

    def begin(buf, lz, ly, lc):
        each(1, A, lambda p: line(buf, lz, p).start())
        cross(buf, ly, z).start()
        core(buf, lc, mj).start()

    def pass_line(buf, lz, ly, lc):
        def body(p):
            zs = (z + p) % A
            line_in(buf, lz, p).wait_recv()
            cross(buf, ly, zs).start()
            core(buf, lc, zs * 2 + y).start()

        each(1, A, body)

    def pass_cross(buf, ly, lc):
        def body(p):
            zs = (z + p) % A
            cross_in(buf, ly, zs).wait_recv()
            core(buf, lc, zs * 2 + 1 - y).start()

        each(0, A, body)

    each(1, T, lambda p: spread(xr, xsem, p).start())
    begin(ir, iz, iy, ic)
    locals_[0].wait()
    begin(tall, tz, ty, tc)

    total = mask.shape[1]
    tile_of = lax.broadcasted_iota(jnp.int32, (TBLOCK, total), 1) // TILE_ROWS
    for b in range(tiles.shape[0]):
        seen = jnp.zeros((TBLOCK, total), F32)
        for j in range(tiles.shape[1]):
            listed = (tile_of == tiles[b : b + 1, j : j + 1]) & (counts[b : b + 1, :] > j)
            seen = jnp.where(listed, 1.0, seen)
        mask[b * TBLOCK : (b + 1) * TBLOCK, :] = seen

    each(1, T, lambda p: spread_in(xr, xsem, p).wait_recv())
    for i in range(T):
        xs[i * rows : (i + 1) * rows, :] = xr[i].astype(F32)
    states = xs[...]
    center = states - jnp.mean(states, axis=-1, keepdims=True)
    spread_sq = jnp.mean(center * center, axis=-1, keepdims=True)
    normed = (center * lax.rsqrt(spread_sq + 1e-06)).astype(BF16)
    locals_[1].wait()
    pre = dot(normed, fc1[...])
    hidden = (0.5 * pre * (1.0 + lax.erf(pre * (0.5**0.5)))).astype(BF16)
    locals_[2].wait()
    partial_value = dot(hidden, fc2[...])
    for i in range(T):
        part[i] = partial_value[i * rows : (i + 1) * rows, :]
    each(1, T, lambda p: part_out(p).start())
    pass_line(ir, iz, iy, ic)
    each(1, T, lambda p: part_in(p).wait_recv())
    total_value = lax.fori_loop(
        1, T, lambda p, acc: acc + partr[(me + p) % T], part[me]
    )
    er[me] = (patches[...].astype(F32) + total_value).astype(BF16)
    each(1, T, lambda p: spread(er, esem, p).start())
    pass_cross(ir, iy, ic)
    pass_line(tall, tz, ty, tc)

    each(0, J, lambda j: core_in(ir, ic, j).wait_recv())
    for i in range(T):
        xs[i * rows : (i + 1) * rows, :] = xr[i].astype(F32)
        feats[i * rows : (i + 1) * rows, :] = ir[i].astype(F32)
    locals_[3].wait()
    image = jnp.zeros((group, width), F32)
    chunks = inter.shape[1] // dv
    for k in range(chunks):
        image += dot(
            feats[:, k * dv : (k + 1) * dv].astype(BF16), proj[(k + 1) * dv : (k + 2) * dv, :]
        )
    each(1, T, lambda p: spread_in(er, esem, p).wait_recv())
    for i in range(T):
        xs[i * rows : (i + 1) * rows, :] = er[i].astype(F32)
    image += dot(xs[...].astype(BF16), proj[0:dv, :])
    img[sec] = image.astype(BF16)
    swap = remote(img.at[sec], img.at[sec], msem.at[0], msem.at[1], section=1 - sec)
    swap_in = remote(img.at[1 - sec], img.at[1 - sec], msem.at[0], msem.at[1], section=1 - sec)
    swap.start()
    pass_cross(tall, ty, tc)
    locals_[4].wait()
    swap_in.wait_recv()

    part_rows = total // G
    image_all = jnp.concatenate([img[0], img[1]], axis=0)

    def head_terms(h):
        k = dot(image_all, kvw[:, pl.ds(pl.multiple_of(h * HD, HD), HD)])
        v = dot(image_all, kvw[:, pl.ds(pl.multiple_of((KV_HEADS + h) * HD, HD), HD)])
        for r in range(G):
            at = slice(r * part_rows, (r + 1) * part_rows)
            kvp[r % 2, h * (G // 2) + r // 2, :, 0:HD] = k[at]
            kvp[r % 2, h * (G // 2) + r // 2, :, HD : 2 * HD] = v[at]

    each(0, KV_HEADS, head_terms)
    kv_pair = remote(kvp.at[1 - c], kcr, kc.at[0], kc.at[1], tensor=pair)
    kv_pair.start()

    each(0, J, lambda j: core_in(tall, tc, j).wait_recv())
    locals_[5].wait()
    query[...] = jnp.zeros_like(query)

    def query_term(b):
        query[...] += dot(tall[b], qw[pl.ds(pl.multiple_of(b * width, width), width), :])

    kv_pair.wait_recv()

    def kv_out(p):
        j = (mj + p) % J
        return remote(kvp.at[c, j], kzr.at[mj], kz.at[0, p], kz.at[1, mj], tensor=j * 2 + c)

    def kv_in(p):
        j = (mj + p) % J
        return remote(kvp.at[c, j], kzr.at[j], kz.at[0, p], kz.at[1, j], tensor=j * 2 + c)

    def kv_send(p):
        j = (mj + p) % J
        kvp[c, j] = kvp[c, j] + kcr[j]
        kv_out(p).start()

    each(1, J, kv_send)
    each(0, T, query_term)
    each(1, J, lambda p: kv_in(p).wait_recv())
    kv_own = lax.fori_loop(
        1, J, lambda p, acc: acc + kzr[(mj + p) % J], kvp[c, mj] + kcr[mj]
    )
    place = me % G
    kvh[place] = kv_own.astype(BF16)

    def share(p):
        to = (me // G) * G + (place + p) % G
        return remote(kvh.at[place], kvh.at[place], kg.at[0, p], kg.at[1, place], tensor=to)

    def share_in(p):
        r = (place + p) % G
        return remote(kvh.at[r], kvh.at[r], kg.at[0, p], kg.at[1, r], tensor=(me // G) * G + r)

    each(1, G, lambda p: share(p).start())
    for h in range(hl):
        q = query[:, h * HD : (h + 1) * HD]
        query[:, h * HD : (h + 1) * HD] = rms_scale(q, qgain[...])
    each(1, G, lambda p: share_in(p).wait_recv())

    kv_all = jnp.concatenate([kvh[r] for r in range(G)], axis=0)
    keys = rms_scale(kv_all[:, 0:HD].astype(F32), kgain[...]).astype(BF16)
    values = kv_all[:, HD : 2 * HD]
    for h in range(hl):
        q = query[:, h * HD : (h + 1) * HD].astype(BF16)
        scores = lax.dot_general(
            q, keys, (((1,), (1,)), ((), ())), preferred_element_type=F32
        ) * (1.0 / HD**0.5)
        scores = jnp.where(mask[...] > 0.5, scores, -1e30)
        weights = jnp.exp(scores - jnp.max(scores, axis=-1, keepdims=True))
        probs = (weights / jnp.sum(weights, axis=-1, keepdims=True)).astype(BF16)
        att[:, h * HD : (h + 1) * HD] = dot(probs, values).astype(BF16)

    locals_[6].wait()

    def columns(zs, yy, cc):
        first = pl.multiple_of(((zs * 2 + yy) * 2 + cc) * width, width)
        return dot(att[...], ow[:, pl.ds(first, width)])

    def pair_out(k):
        return remote(ocs.at[k], ocr.at[k], oc.at[0, k], oc.at[1, k], tensor=pair)

    def across_out(k):
        return remote(oys.at[k], oyr.at[k], oy.at[0, k], oy.at[1, k], tensor=across)

    def line_out(k):
        zs = (z + 1 + k) % A
        return remote(
            ozs.at[k], ozr.at[k], oz.at[0, k], oz.at[1, k], tensor=zs * 4 + y * 2 + c
        )

    def terms_pair(k):
        zs = (z + 1 + k) % A
        for yy in range(2):
            ocs[k, yy] = columns(zs, yy, 1 - c)
        pair_out(k).start()

    def terms_own(k):
        zs = (z + 1 + k) % A
        for yy in range(2):
            own[k, yy] = columns(zs, yy, c)
        pair_out(k).wait_recv()
        oys[k] = (own[k, 1 - y] + ocr[k, 1 - y]).astype(BF16)
        across_out(k).start()

    each(0, A, terms_pair)
    each(0, A, terms_own)

    def terms_line(k):
        across_out(k).wait_recv()
        ozs[k] = (own[k, y] + ocr[k, y] + oyr[k].astype(F32)).astype(BF16)
        line_out(k).start()

    each(0, A - 1, terms_line)
    across_out(A - 1).wait_recv()
    branch = own[A - 1, y] + ocr[A - 1, y] + oyr[A - 1].astype(F32)
    each(0, A - 1, lambda k: line_out(k).wait_recv())
    for k in range(A - 1):
        branch += ozr[k].astype(F32)
    out[...] = (tall[me].astype(F32) + jnp.tanh(gate[...]) * branch).astype(BF16)

    def sent_all(p):
        spread(xr, xsem, p).wait_send()
        part_out(p).wait_send()
        spread(er, esem, p).wait_send()

    each(1, T, sent_all)

    def sent_line(p):
        line(ir, iz, p).wait_send()
        line(tall, tz, p).wait_send()
        line_out(p - 1).wait_send()

    each(1, A, sent_line)

    def sent_cross(zs):
        cross(ir, iy, zs).wait_send()
        cross(tall, ty, zs).wait_send()
        pair_out(zs).wait_send()
        across_out(zs).wait_send()

    each(0, A, sent_cross)

    def sent_core(j):
        core(ir, ic, j).wait_send()
        core(tall, tc, j).wait_send()

    each(0, J, sent_core)
    swap.wait_send()
    kv_pair.wait_send()
    each(1, J, lambda p: kv_out(p).wait_send())
    each(1, G, lambda p: share(p).wait_send())


def shards(T, *arrays):
    (
        patches,
        intermediate,
        fc1_weight,
        fc2_weight,
        projector,
        text,
        query_weight,
        kv_weight,
        query_gain,
        key_gain,
        out_weight,
        attn_gate,
        tile_list,
        list_count,
    ) = arrays
    A, J, G = T // 4, T // 2, T // KV_HEADS
    rows, dv = patches.shape
    inter_w = intermediate.shape[1]
    group = rows * T
    total = group * 2
    _, txt, width = text.shape
    vm = pltpu.VMEM
    pairs = lambda n: pltpu.SemaphoreType.DMA((2, n))
    scratch = [
        vm(fc1_weight.shape, BF16),
        vm(fc2_weight.shape, BF16),
        vm(projector.shape, BF16),
        vm(query_weight.shape[1:], BF16),
        vm(kv_weight.shape[1:], BF16),
        vm(out_weight.shape[1:], BF16),
        vm((T, rows, dv), BF16),
        vm((group, dv), F32),
        vm((T, rows, dv), F32),
        vm((T, rows, dv), F32),
        vm((T, rows, dv), BF16),
        vm((T, rows, inter_w), BF16),
        vm((group, inter_w), F32),
        vm((2, group, width), BF16),
        vm((T, txt, width), BF16),
        vm((txt, width), F32),
        vm((2, J, total // G, 2 * HD), F32),
        vm((J, total // G, 2 * HD), F32),
        vm((J, total // G, 2 * HD), F32),
        vm((G, total // G, 2 * HD), BF16),
        vm((txt, total), F32),
        vm((txt, width), BF16),
        vm((A, 2, txt, width), F32),
        vm((A, 2, txt, width), F32),
        vm((A, 2, txt, width), F32),
        vm((A, txt, width), BF16),
        vm((A, txt, width), BF16),
        vm((A - 1, txt, width), BF16),
        vm((A - 1, txt, width), BF16),
        pltpu.SemaphoreType.DMA((7,)),
        pairs(T),
        pairs(T),
        pairs(T),
        pairs(A),
        pairs(A),
        pairs(J),
        pairs(A),
        pairs(A),
        pairs(J),
        pltpu.SemaphoreType.DMA((2,)),
        pltpu.SemaphoreType.DMA((2,)),
        pairs(J),
        pairs(G),
        pairs(A),
        pairs(A),
        pairs(A),
    ]
    mixed = pl.pallas_call(
        functools.partial(kernel, T),
        out_shape=jax.ShapeDtypeStruct((txt, width), BF16),
        in_specs=[pl.BlockSpec(memory_space=pltpu.VMEM)] * 7
        + [pl.BlockSpec(memory_space=pl.ANY)] * 7,
        out_specs=pl.BlockSpec(memory_space=pltpu.VMEM),
        scratch_shapes=scratch,
        compiler_params=pltpu.CompilerParams(
            collective_id=0, has_side_effects=True, vmem_limit_bytes=60 * 1024 * 1024
        ),
        name="tail",
    )(
        patches,
        intermediate,
        query_gain,
        key_gain,
        attn_gate.reshape(1, 1),
        tile_list[0],
        list_count.reshape(-1, 1),
        text[0],
        fc1_weight,
        fc2_weight,
        projector,
        query_weight[0],
        kv_weight[0],
        out_weight[0],
    )
    return mixed[None]


def solution(mesh):
    placed = (
        P(("section", "tensor"), None),
        P(("section", "tensor"), None),
        P(None, "tensor"),
        P("tensor", None),
        P(None, "tensor"),
        P("section", None, "tensor"),
        P("section", None, "tensor"),
        P("section", "tensor", None),
        P("section", None),
        P("section", None),
        P("section", "tensor", None),
        P("section"),
        P("section", None, None),
        P("section", None),
    )
    return jax.shard_map(
        functools.partial(shards, mesh.shape["tensor"]),
        mesh=mesh,
        in_specs=placed,
        out_specs=P("section", None, "tensor"),
        check_vma=False,
    )
```

time: 372 us -> 129 us (0.35)
  waiting for transfers between devices: 242 us -> 0 us
  Pallas kernels: 0 us -> 123 us
  blocking collectives: 71 us -> 0 us
  matrix products: 27.4 us -> 0 us
  between operations: 14 us -> 0.66 us
  local copies, waits for them, and re-layouts: 13.1 us -> 5.2 us
    reduce_scatter x2 -> x0, waiting for transfers between devices: 148 us -> none  [the longest x1 102 us: shards(): branch = lax.psum_scatter(terms, 'tensor', scatter_dimension=1, tiled=True)]
    pallas_call x0 -> x1, Pallas kernels: none -> 123 us  [shards(): pl.pallas_call(functools.partial(kernel, T), out_shape=jax.ShapeDtypeStru...]
    all_gather x4 -> x0, blocking collectives: 71 us -> none  [the longest x1 23.9 us: shards(): lax.all_gather(patches, 'tensor', axis=0, tiled=True)]
    psum x1 -> x0, waiting for transfers between devices: 60.7 us -> none  [shards(): encoded = (states + lax.psum(partial_value, 'tensor')).astype(jnp.bfloat16)]
    all_gather x1 -> x0, waiting for transfers between devices: 33 us -> none  [shards(): full_text = lax.all_gather(text[0], 'tensor', axis=1, tiled=True)]
    dot_general x8 -> x0, matrix products: 27.4 us -> none  [the longest x1 8.99 us: shards(): terms = jnp.dot(attended, out_weight[0], preferred_element_type=jnp.float32)]
    dot_general x1 -> x0, local copies, waits for them, and re-layouts: 11.4 us -> none  [shards(): jnp.dot(full_text, query_weight[0], preferred_element_type=jnp.float32)]
  transfers between devices with their start and end apart: 4 -> 0, of which waited for: 4 -> 0; matrix products, arithmetic and copies ran while one was open for 5% -> 0% of each run, Pallas kernels for 0% -> 0%
where the time goes in v1:
time: 129 us
  Pallas kernels  123 us (95%)
  local copies, waits for them, and re-layouts  5.2 us (4%)
    pallas_call x1, Pallas kernels, shards(): pl.pallas_call(functools.partial(kernel, T), out_shape=jax.ShapeDtypeStru...  123 us
    unnamed x2, local copies, waits for them, and re-layouts  3.89 us

profile of v1, /device:TPU:0, one launch (start us, length us, event | category | flops | bytes accessed | tf_op | source)
XLA Modules:
  0.0 128.5 jit_solution(10987049281052019067)
XLA Ops:
  0.7 1.3 %copy.15.counts = s32[4,1]{1,0:T(4,128)} copy(s32[4,1]{0,1:T(1,128)} %bitcast.15) | data formatting | bytes 32 | tf_op jit(solution)/shard_map/reshape | solution.py:533
  2.0 2.2 %copy.16.fc1_hbm = bf16[1280,320]{1,0:T(8,128)(2,1)} copy(bf16[1280,320]{0,1:T(8,128)(2,1)} %param.16) | data formatting | bytes 1638400 | tf_op args[2]
  4.2 122.7 %tail.1 = bf16[256,512]{1,0:T(8,128)(2,1)} custom-call(bf16[4,1280]{1,0:T(4,128)(2,1)} %patches.1, bf16[4,6400]{1,0:T(4,128)(2,1)} %inter.1, f32[1,128]{1,0:T(1,128)} %qgain.1, f32[1,128]{1,0:T(1,128)} %kgain.1, f32[1,1]{1,0:T(1,128)} %bitcast.8.gate, s32[4,4]{1,0:T(4,128)} %bitcast.14, s32[4,1]{1,0:T(4,128)} %copy.15.counts, bf16[256,512]{1,0:T(8,128)(2,1)} %bitcast.13, ...), custom_call_target="tpu_custom_call" | custom-call | tf_op jit(solution)/shard_map/tail/pallas_call | solution.py:515
  126.9 1.7 %copy.19 = bf16[1,256,512]{2,1,0:T(8,128)(2,1)} copy(bf16[1,256,512]{2,1,0:T(8,128)(2,1)} %bitcast.12) | data formatting | bytes 524288

commit v2 on v1

--- a/solution.py
+++ b/solution.py
@@ -12,6 +12,7 @@
 HD = 128
 TILE_ROWS = 64
 TBLOCK = 64
+CHUNKS = 4
 F32 = jnp.float32
 BF16 = jnp.bfloat16
 
@@ -223,17 +224,67 @@
 
         each(0, A, body)
 
+    step = txt // CHUNKS
+
+    def text_copy(b, ch, sem, send, recv, to):
+        rows_of = tall.at[b, pl.ds(ch * step, step), :]
+        return remote(
+            rows_of, rows_of, sem.at[0, send * CHUNKS + ch], sem.at[1, recv * CHUNKS + ch], tensor=to
+        )
+
+    def text_line(ch, p):
+        return text_copy(me, ch, tz, p, z, ((z + p) % A) * 4 + y * 2 + c)
+
+    def text_line_in(ch, p):
+        zs = (z + p) % A
+        src = zs * 4 + y * 2 + c
+        return text_copy(src, ch, tz, p, zs, src)
+
+    def text_cross(ch, zs):
+        return text_copy(zs * 4 + y * 2 + c, ch, ty, zs, zs, across)
+
+    def text_cross_in(ch, zs):
+        return text_copy(zs * 4 + (1 - y) * 2 + c, ch, ty, zs, zs, across)
+
+    def text_core(ch, j):
+        return text_copy(j * 2 + c, ch, tc, j, j, pair)
+
+    def text_core_in(ch, j):
+        return text_copy(j * 2 + 1 - c, ch, tc, j, j, pair)
+
+    def text_begin(ch):
+        each(1, A, lambda p: text_line(ch, p).start())
+        text_cross(ch, z).start()
+        text_core(ch, mj).start()
+
+    def text_pass_line(ch):
+        def body(p):
+            zs = (z + p) % A
+            text_line_in(ch, p).wait_recv()
+            text_cross(ch, zs).start()
+            text_core(ch, zs * 2 + y).start()
+
+        each(1, A, body)
+
+    def text_pass_cross(ch):
+        def body(p):
+            zs = (z + p) % A
+            text_cross_in(ch, zs).wait_recv()
+            text_core(ch, zs * 2 + 1 - y).start()
+
+        each(0, A, body)
+
     each(1, T, lambda p: spread(xr, xsem, p).start())
     begin(ir, iz, iy, ic)
     locals_[0].wait()
-    begin(tall, tz, ty, tc)
+    text_begin(0)
 
     total = mask.shape[1]
     tile_of = lax.broadcasted_iota(jnp.int32, (TBLOCK, total), 1) // TILE_ROWS
     for b in range(tiles.shape[0]):
         seen = jnp.zeros((TBLOCK, total), F32)
         for j in range(tiles.shape[1]):
-            listed = (tile_of == tiles[b : b + 1, j : j + 1]) & (counts[b : b + 1, :] > j)
+            listed = (tile_of == tiles[b : b + 1, j : j + 1]) & (counts[:, b : b + 1] > j)
             seen = jnp.where(listed, 1.0, seen)
         mask[b * TBLOCK : (b + 1) * TBLOCK, :] = seen
 
@@ -245,13 +296,17 @@
     spread_sq = jnp.mean(center * center, axis=-1, keepdims=True)
     normed = (center * lax.rsqrt(spread_sq + 1e-06)).astype(BF16)
     locals_[1].wait()
-    pre = dot(normed, fc1[...])
+    pre = lax.dot_general(
+        normed, fc1[...], (((1,), (1,)), ((), ())), preferred_element_type=F32
+    )
     hidden = (0.5 * pre * (1.0 + lax.erf(pre * (0.5**0.5)))).astype(BF16)
     locals_[2].wait()
     partial_value = dot(hidden, fc2[...])
     for i in range(T):
         part[i] = partial_value[i * rows : (i + 1) * rows, :]
     each(1, T, lambda p: part_out(p).start())
+    text_begin(1)
+    text_pass_line(0)
     pass_line(ir, iz, iy, ic)
     each(1, T, lambda p: part_in(p).wait_recv())
     total_value = lax.fori_loop(
@@ -259,8 +314,9 @@
     )
     er[me] = (patches[...].astype(F32) + total_value).astype(BF16)
     each(1, T, lambda p: spread(er, esem, p).start())
+    text_begin(2)
+    text_pass_line(1)
     pass_cross(ir, iy, ic)
-    pass_line(tall, tz, ty, tc)
 
     each(0, J, lambda j: core_in(ir, ic, j).wait_recv())
     for i in range(T):
@@ -281,7 +337,9 @@
     swap = remote(img.at[sec], img.at[sec], msem.at[0], msem.at[1], section=1 - sec)
     swap_in = remote(img.at[1 - sec], img.at[1 - sec], msem.at[0], msem.at[1], section=1 - sec)
     swap.start()
-    pass_cross(tall, ty, tc)
+    text_begin(3)
+    text_pass_line(2)
+    text_pass_cross(0)
     locals_[4].wait()
     swap_in.wait_recv()
 
@@ -300,9 +358,9 @@
     kv_pair = remote(kvp.at[1 - c], kcr, kc.at[0], kc.at[1], tensor=pair)
     kv_pair.start()
 
-    each(0, J, lambda j: core_in(tall, tc, j).wait_recv())
-    locals_[5].wait()
-    query[...] = jnp.zeros_like(query)
+    text_pass_line(3)
+    text_pass_cross(1)
+
 
     def query_term(b):
         query[...] += dot(tall[b], qw[pl.ds(pl.multiple_of(b * width, width), width), :])
@@ -323,6 +381,12 @@
         kv_out(p).start()
 
     each(1, J, kv_send)
+    for ch in range(2, CHUNKS):
+        text_pass_cross(ch)
+    for ch in range(CHUNKS):
+        each(0, J, lambda j, ch=ch: text_core_in(ch, j).wait_recv())
+    locals_[5].wait()
+    query[...] = jnp.zeros_like(query)
     each(0, T, query_term)
     each(1, J, lambda p: kv_in(p).wait_recv())
     kv_own = lax.fori_loop(
@@ -415,14 +479,16 @@
 
     def sent_line(p):
         line(ir, iz, p).wait_send()
-        line(tall, tz, p).wait_send()
+        for ch in range(CHUNKS):
+            text_line(ch, p).wait_send()
         line_out(p - 1).wait_send()
 
     each(1, A, sent_line)
 
     def sent_cross(zs):
         cross(ir, iy, zs).wait_send()
-        cross(tall, ty, zs).wait_send()
+        for ch in range(CHUNKS):
+            text_cross(ch, zs).wait_send()
         pair_out(zs).wait_send()
         across_out(zs).wait_send()
 
@@ -430,7 +496,8 @@
 
     def sent_core(j):
         core(ir, ic, j).wait_send()
-        core(tall, tc, j).wait_send()
+        for ch in range(CHUNKS):
+            text_core(ch, j).wait_send()
 
     each(0, J, sent_core)
     swap.wait_send()
@@ -465,7 +532,7 @@
     vm = pltpu.VMEM
     pairs = lambda n: pltpu.SemaphoreType.DMA((2, n))
     scratch = [
-        vm(fc1_weight.shape, BF16),
+        vm(fc1_weight.shape[::-1], BF16),
         vm(fc2_weight.shape, BF16),
         vm(projector.shape, BF16),
         vm(query_weight.shape[1:], BF16),
@@ -498,9 +565,9 @@
         pairs(T),
         pairs(T),
         pairs(T),
-        pairs(A),
-        pairs(A),
-        pairs(J),
+        pairs(A * CHUNKS),
+        pairs(A * CHUNKS),
+        pairs(J * CHUNKS),
         pairs(A),
         pairs(A),
         pairs(J),
@@ -530,9 +597,9 @@
         key_gain,
         attn_gate.reshape(1, 1),
         tile_list[0],
-        list_count.reshape(-1, 1),
+        list_count,
         text[0],
-        fc1_weight,
+        fc1_weight.T,
         fc2_weight,
         projector,
         query_weight[0],

time: 129 us -> 107 us (0.83)
  Pallas kernels: 123 us -> 104 us
  local copies, waits for them, and re-layouts: 5.2 us -> 1.67 us
    pallas_call x1, Pallas kernels: 123 us -> 104 us  [shards(): pl.pallas_call(functools.partial(kernel, T), out_shape=jax.ShapeDtypeStru...]
    unnamed x2 -> x1, local copies, waits for them, and re-layouts: 3.89 us -> 1.67 us
    reshape x1 -> x0, local copies, waits for them, and re-layouts: 1.31 us -> none  [shards(): list_count.reshape(-1, 1)]
where the time goes in v2:
time: 107 us; the launch traced here: 106 us
  Pallas kernels  104 us (97%)
  local copies, waits for them, and re-layouts  1.67 us (2%)
    pallas_call x1, Pallas kernels, shards(): pl.pallas_call(functools.partial(kernel, T), out_shape=jax.ShapeDtypeStru...  104 us

profile of v2, /device:TPU:0, one launch (start us, length us, event | category | flops | bytes accessed | tf_op | source)
XLA Modules:
  0.0 106.5 jit_solution(6306690665896637021)
XLA Ops:
  0.7 104.2 %tail.1 = bf16[256,512]{1,0:T(8,128)(2,1)} custom-call(bf16[4,1280]{1,0:T(4,128)(2,1)} %patches.1, bf16[4,6400]{1,0:T(4,128)(2,1)} %inter.1, f32[1,128]{1,0:T(1,128)} %qgain.1, f32[1,128]{1,0:T(1,128)} %kgain.1, f32[1,1]{1,0:T(1,128)} %bitcast.8.gate, s32[4,4]{1,0:T(4,128)} %bitcast.15, s32[1,4]{1,0:T(1,128)} %counts.1, bf16[256,512]{1,0:T(8,128)(2,1)} %bitcast.14, ...), custom_call_target="tpu_custom_call" | custom-call | tf_op jit(solution)/shard_map/tail/pallas_call | solution.py:582
  104.8 1.7 %copy.17 = bf16[1,256,512]{2,1,0:T(8,128)(2,1)} copy(bf16[1,256,512]{2,1,0:T(8,128)(2,1)} %bitcast.12) | data formatting | bytes 524288

commit v3 on v2

--- a/solution.py
+++ b/solution.py
@@ -13,6 +13,8 @@
 TILE_ROWS = 64
 TBLOCK = 64
 CHUNKS = 4
+CUTS = 2
+LAG = 3
 F32 = jnp.float32
 BF16 = jnp.bfloat16
 
@@ -424,51 +426,66 @@
 
     locals_[6].wait()
 
-    def columns(zs, yy, cc):
+    S = A * CUTS
+    half = txt // CUTS
+
+    def columns(s, yy, cc):
+        zs = (z + 1 + s // CUTS) % A
         first = pl.multiple_of(((zs * 2 + yy) * 2 + cc) * width, width)
-        return dot(att[...], ow[:, pl.ds(first, width)])
-
-    def pair_out(k):
-        return remote(ocs.at[k], ocr.at[k], oc.at[0, k], oc.at[1, k], tensor=pair)
-
-    def across_out(k):
-        return remote(oys.at[k], oyr.at[k], oy.at[0, k], oy.at[1, k], tensor=across)
-
-    def line_out(k):
-        zs = (z + 1 + k) % A
+        at = pl.multiple_of((s % CUTS) * half, half)
+        return dot(att[pl.ds(at, half), :], ow[:, pl.ds(first, width)])
+
+    def pair_out(s):
+        return remote(ocs.at[s], ocr.at[s], oc.at[0, s], oc.at[1, s], tensor=pair)
+
+    def across_out(s):
+        return remote(oys.at[s], oyr.at[s], oy.at[0, s], oy.at[1, s], tensor=across)
+
+    def line_out(s):
+        zs = (z + 1 + s // CUTS) % A
         return remote(
-            ozs.at[k], ozr.at[k], oz.at[0, k], oz.at[1, k], tensor=zs * 4 + y * 2 + c
+            ozs.at[s], ozr.at[s], oz.at[0, s], oz.at[1, s], tensor=zs * 4 + y * 2 + c
         )
 
-    def terms_pair(k):
-        zs = (z + 1 + k) % A
+    def terms_pair(s):
         for yy in range(2):
-            ocs[k, yy] = columns(zs, yy, 1 - c)
-        pair_out(k).start()
-
-    def terms_own(k):
-        zs = (z + 1 + k) % A
+            ocs[s, yy] = columns(s, yy, 1 - c)
+        pair_out(s).start()
+
+    def terms_own(s):
         for yy in range(2):
-            own[k, yy] = columns(zs, yy, c)
-        pair_out(k).wait_recv()
-        oys[k] = (own[k, 1 - y] + ocr[k, 1 - y]).astype(BF16)
-        across_out(k).start()
-
-    each(0, A, terms_pair)
-    each(0, A, terms_own)
-
-    def terms_line(k):
-        across_out(k).wait_recv()
-        ozs[k] = (own[k, y] + ocr[k, y] + oyr[k].astype(F32)).astype(BF16)
-        line_out(k).start()
-
-    each(0, A - 1, terms_line)
-    across_out(A - 1).wait_recv()
-    branch = own[A - 1, y] + ocr[A - 1, y] + oyr[A - 1].astype(F32)
-    each(0, A - 1, lambda k: line_out(k).wait_recv())
-    for k in range(A - 1):
-        branch += ozr[k].astype(F32)
-    out[...] = (tall[me].astype(F32) + jnp.tanh(gate[...]) * branch).astype(BF16)
+            own[s, yy] = columns(s, yy, c)
+        pair_out(s).wait_recv()
+        oys[s] = (own[s, 1 - y] + ocr[s, 1 - y]).astype(BF16)
+        across_out(s).start()
+
+    def terms_both(s):
+        terms_pair(s)
+        terms_own(s - 1)
+
+    def terms_line(s):
+        across_out(s).wait_recv()
+        ozs[s] = (own[s, y] + ocr[s, y] + oyr[s].astype(F32)).astype(BF16)
+        line_out(s).start()
+
+    def terms_three(s):
+        terms_both(s)
+        terms_line(s - LAG)
+
+    terms_pair(0)
+    each(1, LAG, terms_both)
+    each(LAG, S, terms_three)
+    terms_own(S - 1)
+    each(S - LAG, S - CUTS, terms_line)
+    for r in range(CUTS):
+        s = S - CUTS + r
+        at = slice(r * half, (r + 1) * half)
+        across_out(s).wait_recv()
+        branch = own[s, y] + ocr[s, y] + oyr[s].astype(F32)
+        each(0, A - 1, lambda k, r=r: line_out(k * CUTS + r).wait_recv())
+        for k in range(A - 1):
+            branch += ozr[k * CUTS + r].astype(F32)
+        out[at, :] = (tall[me, at, :].astype(F32) + jnp.tanh(gate[...]) * branch).astype(BF16)
 
     def sent_all(p):
         spread(xr, xsem, p).wait_send()
@@ -481,7 +498,8 @@
         line(ir, iz, p).wait_send()
         for ch in range(CHUNKS):
             text_line(ch, p).wait_send()
-        line_out(p - 1).wait_send()
+        for r in range(CUTS):
+            line_out((p - 1) * CUTS + r).wait_send()
 
     each(1, A, sent_line)
 
@@ -489,8 +507,9 @@
         cross(ir, iy, zs).wait_send()
         for ch in range(CHUNKS):
             text_cross(ch, zs).wait_send()
-        pair_out(zs).wait_send()
-        across_out(zs).wait_send()
+        for r in range(CUTS):
+            pair_out(zs * CUTS + r).wait_send()
+            across_out(zs * CUTS + r).wait_send()
 
     each(0, A, sent_cross)
 
@@ -554,13 +573,13 @@
         vm((G, total // G, 2 * HD), BF16),
         vm((txt, total), F32),
         vm((txt, width), BF16),
-        vm((A, 2, txt, width), F32),
-        vm((A, 2, txt, width), F32),
-        vm((A, 2, txt, width), F32),
-        vm((A, txt, width), BF16),
-        vm((A, txt, width), BF16),
-        vm((A - 1, txt, width), BF16),
-        vm((A - 1, txt, width), BF16),
+        vm((A * CUTS, 2, txt // CUTS, width), F32),
+        vm((A * CUTS, 2, txt // CUTS, width), F32),
+        vm((A * CUTS, 2, txt // CUTS, width), F32),
+        vm((A * CUTS, txt // CUTS, width), BF16),
+        vm((A * CUTS, txt // CUTS, width), BF16),
+        vm(((A - 1) * CUTS, txt // CUTS, width), BF16),
+        vm(((A - 1) * CUTS, txt // CUTS, width), BF16),
         pltpu.SemaphoreType.DMA((7,)),
         pairs(T),
         pairs(T),
@@ -575,9 +594,9 @@
         pltpu.SemaphoreType.DMA((2,)),
         pairs(J),
         pairs(G),
-        pairs(A),
-        pairs(A),
-        pairs(A),
+        pairs(A * CUTS),
+        pairs(A * CUTS),
+        pairs(A * CUTS),
     ]
     mixed = pl.pallas_call(
         functools.partial(kernel, T),

time: 107 us -> 104 us (0.972)
  Pallas kernels: 104 us -> 100 us
    pallas_call x1, Pallas kernels: 104 us -> 100 us  [shards(): pl.pallas_call(functools.partial(kernel, T), out_shape=jax.ShapeDtypeStru...]
where the time goes in v3:
time: 104 us; the launch traced here: 103 us
  Pallas kernels  100 us (96%)
  local copies, waits for them, and re-layouts  1.67 us (2%)
    pallas_call x1, Pallas kernels, shards(): pl.pallas_call(functools.partial(kernel, T), out_shape=jax.ShapeDtypeStru...  100 us

profile of v3, /device:TPU:0, one launch (start us, length us, event | category | flops | bytes accessed | tf_op | source)
XLA Modules:
  0.0 102.8 jit_solution(338324334578540696)
XLA Ops:
  0.7 100.5 %tail.1 = bf16[256,512]{1,0:T(8,128)(2,1)} custom-call(bf16[4,1280]{1,0:T(4,128)(2,1)} %patches.1, bf16[4,6400]{1,0:T(4,128)(2,1)} %inter.1, f32[1,128]{1,0:T(1,128)} %qgain.1, f32[1,128]{1,0:T(1,128)} %kgain.1, f32[1,1]{1,0:T(1,128)} %bitcast.8.gate, s32[4,4]{1,0:T(4,128)} %bitcast.15, s32[1,4]{1,0:T(1,128)} %counts.1, bf16[256,512]{1,0:T(8,128)(2,1)} %bitcast.14, ...), custom_call_target="tpu_custom_call" | custom-call | tf_op jit(solution)/shard_map/tail/pallas_call | solution.py:601
  101.2 1.7 %copy.17 = bf16[1,256,512]{2,1,0:T(8,128)(2,1)} copy(bf16[1,256,512]{2,1,0:T(8,128)(2,1)} %bitcast.12) | data formatting | bytes 524288
